TPU v7x, 32 devices: a whole 2x2x4 slice. The times are simulated.
32 devices in a mesh: node: 8 (over y, x, core), local: 4 (over z).
Axes of the slice: x: 2, y: 2, z: 4, core: 2. Of those that a mesh axis runs over, the one named last changes fastest.
Arguments:
- tokens: bfloat16 [4096, 2048], P(('node', 'local')), may hold values from -6 to 6
- route: int32 [4096, 4], P(('node', 'local')), may hold values from 0 to 63, all different within a row; in each aligned block of 128 rows (0 to 127, 128 to 255, ...) at most 9 rows name the same one
- combine_weights: float32 [4096, 4], P(('node', 'local')), may hold values from 0.05 to 1
- w_gate: bfloat16 [64, 2048, 1408], P('node', None, 'local'), may hold values from -0.125 to 0.125
- w_up: bfloat16 [64, 2048, 1408], P('node', None, 'local'), may hold values from -0.125 to 0.125
- w_down: bfloat16 [64, 1408, 2048], P('node', 'local'), may hold values from -0.15625 to 0.15625
- grad_out: bfloat16 [4096, 2048], P(('node', 'local')), may hold values from -6 to 6
Outputs:
- combined: bfloat16 [4096, 2048], P(('node', 'local'))
- d_tokens: bfloat16 [4096, 2048], P(('node', 'local'))
- d_weights: float32 [4096, 4], P(('node', 'local'))
Inputs may be any that keep to these rules, and one draw needn't show every extreme that they name: `route`: the 4 experts of one token differ; within the 128 tokens of one device no expert is named more than 9 times, and some device names some expert exactly 9 times.
All inputs are finite; a program needn't handle non-finite values.
Results may differ from a plain program's by a relative error of at most 0.012.
Values may be sent and summed in bfloat16 or wider, within the bound.
A program may use at most 192 MiB of HBM per device.

v0:
```python
import jax
import jax.numpy as jnp
from jax import lax
from jax.sharding import PartitionSpec as P

EXPERTS = 64
TOP = 4
CAP = 9


def place_pairs(route):
    flat_routes = route.reshape(-1)
    one_hot = (flat_routes[:, None] == jnp.arange(EXPERTS, dtype=jnp.int32)[None, :]).astype(
        jnp.int32
    )
    earlier = jnp.cumsum(one_hot, axis=0) - one_hot
    slot_rank = jnp.sum(earlier * one_hot, axis=1)
    return flat_routes * CAP + slot_rank


def shards(tokens, route, combine_weights, w_gate, w_up, w_down, grad_out):
    node_count = lax.axis_size("node")
    tok_rows, model_width = tokens.shape
    per_node = w_gate.shape[0]
    pair_rows = tok_rows * TOP
    position = place_pairs(route)
    targets = (jnp.arange(EXPERTS * CAP, dtype=jnp.int32)[:, None] == position[None, :]).astype(
        jnp.bfloat16
    )
    token_targets = targets.reshape(EXPERTS * CAP, tok_rows, TOP).sum(axis=2)
    full_gate, full_up, full_down = (w_gate, w_up, w_down)
    hidden_width = full_gate.shape[2]
    w_inner = jnp.concatenate([full_gate, full_up], axis=2)

    def dispatch(send_rows, worker):
        outgoing = send_rows.reshape(node_count, per_node, CAP, model_width)
        arrived = lax.all_to_all(outgoing, "node", split_axis=0, concat_axis=0, tiled=True)
        return worker(lax.all_gather(arrived[None], "local", axis=0, tiled=True), jnp.int32(0))

    def combine(term_fn):
        summed = lax.psum_scatter(
            term_fn(jnp.int32(0), 1 * lax.axis_size("local")).astype(jnp.bfloat16),
            "local",
            scatter_dimension=0,
            tiled=True,
        ).astype(jnp.float32)
        returned = lax.all_to_all(
            summed[0].astype(jnp.bfloat16), "node", split_axis=0, concat_axis=0, tiled=True
        )
        return returned.reshape(EXPERTS * CAP, model_width)

    send_tokens = jnp.dot(token_targets, tokens, preferred_element_type=jnp.float32).astype(
        jnp.bfloat16
    )

    def forward_work(block_rows, first_row):
        return jnp.einsum(
            "abecd,edh->abech", block_rows, w_inner, preferred_element_type=jnp.float32
        )

    gate_up = dispatch(send_tokens, forward_work)
    hidden = (jax.nn.silu(gate_up[..., :hidden_width]) * gate_up[..., hidden_width:]).astype(
        jnp.bfloat16
    )

    def down_term(first_row, row_count):
        return jnp.einsum("abech,ehd->abecd", hidden, full_down, preferred_element_type=jnp.float32)

    expert_out = combine(down_term)
    pair_view = expert_out[position].reshape(tok_rows, TOP, model_width)
    combined = jnp.sum(combine_weights[:, :, None] * pair_view.astype(jnp.float32), axis=1).astype(
        jnp.bfloat16
    )
    d_weights = jnp.einsum("tkd,td->tk", pair_view, grad_out, preferred_element_type=jnp.float32)
    grad_pairs = (
        (combine_weights[:, :, None] * grad_out[:, None, :].astype(jnp.float32))
        .astype(jnp.bfloat16)
        .reshape(pair_rows, model_width)
    )
    send_grads = jnp.dot(targets, grad_pairs, preferred_element_type=jnp.float32).astype(
        jnp.bfloat16
    )

    def backward_work(block_rows, first_row):
        d_hidden = jnp.einsum(
            "abecd,ehd->abech", block_rows, full_down, preferred_element_type=jnp.float32
        )
        gate_val = gate_up[..., :hidden_width]
        up_val = gate_up[..., hidden_width:]
        sigmoid_gate = jax.nn.sigmoid(gate_val)
        d_gate = d_hidden * up_val * sigmoid_gate * (1.0 + gate_val * (1.0 - sigmoid_gate))
        d_up = d_hidden * gate_val * sigmoid_gate
        return jnp.concatenate([d_gate.astype(jnp.bfloat16), d_up.astype(jnp.bfloat16)], axis=-1)

    d_inner = dispatch(send_grads, backward_work)

    def back_term(first_row, row_count):
        return jnp.einsum("abech,edh->abecd", d_inner, w_inner, preferred_element_type=jnp.float32)

    d_rows = combine(back_term)
    d_pairs = d_rows[position].reshape(tok_rows, TOP, model_width)
    d_tokens = jnp.sum(d_pairs.astype(jnp.float32), axis=1).astype(jnp.bfloat16)
    return (combined, d_tokens, d_weights)


def solution(mesh):
    return jax.shard_map(
        shards,
        mesh=mesh,
        in_specs=(
            P(("node", "local"), None),
            P(("node", "local"), None),
            P(("node", "local"), None),
            P("node", None, "local"),
            P("node", None, "local"),
            P("node", "local", None),
            P(("node", "local"), None),
        ),
        out_specs=(
            P(("node", "local"), None),
            P(("node", "local"), None),
            P(("node", "local"), None),
        ),
        check_vma=False,
    )
```

profile of v0, /device:TPU:0, one launch (start us, length us, event | category | flops | bytes accessed | tf_op | source)
XLA Modules:
  0.0 852.6 jit_solution(9985631156591641046)
XLA Ops:
  7.2 0.8 copy.39
  8.1 0.1 eq.50
  8.2 0.1 eq.46
  8.3 1.2 reduce-window.6
  9.5 0.2 slice_reduce_fusion
  9.8 0.1 fusion.23
  10.0 0.6 broadcast_multiply_fusion
  10.7 0.1 fusion.19
  10.9 0.8 convolution_convert_fusion.1
  11.7 2.8 reshape.97
  14.5 3.9 copy.44
  18.3 34.5 %all_to_all.20 = bf16[8,8,9,2048]{3,1,2,0:T(8,128)(2,1)} all-to-all(bf16[8,8,9,2048]{3,1,2,0:T(8,128)(2,1)S(1)} %copy.44), channel_id=1, replica_groups=mesh['node'=8,'local'=4] {'node'}, dimensions={0} | all-to-all | bytes 4718592 | tf_op jit(solution)/shard_map/all_to_all | solution.py:37
  52.9 0.1 copy.38
  53.1 3.0 mul.91
  56.1 5.5 mul.92
  61.6 4.0 convolution_convert_fusion
  65.6 2.8 reshape.100
  68.4 3.8 copy.49
  72.2 32.6 %all_to_all.21 = bf16[8,8,9,2048]{3,1,2,0:T(8,128)(2,1)} all-to-all(bf16[8,8,9,2048]{3,1,2,0:T(8,128)(2,1)S(1)} %copy.49), channel_id=1, replica_groups=mesh['node'=8,'local'=4] {'node'}, dimensions={0} | all-to-all | bytes 4718592 | tf_op jit(solution)/shard_map/all_to_all | solution.py:37
  104.9 0.2 reduce-scatter.5.cloned.1.call-start
  105.1 114.1 %all-gather.5.cloned.1.call-done = bf16[32,8,9,2048]{3,1,2,0:T(8,128)(2,1)} async-done(((bf16[8,8,9,2048]{3,1,2,0:T(8,128)(2,1)}), bf16[32,8,9,2048]{3,1,2,0:T(8,128)(2,1)}) %all-gather.5.cloned.1.call-update) | async-done | bytes 9437200 | tf_op jit(solution)/shard_map/all_gather | solution.py:38
  219.1 11.0 %copy.45 = bf16[32,8,9,2048]{3,2,0,1:T(8,128)(2,1)} copy(bf16[32,8,9,2048]{3,1,2,0:T(8,128)(2,1)} %all-gather.5.cloned.1.call-done) | data formatting | bytes 18874368 | tf_op jit(solution)/shard_map/all_gather | solution.py:38
  230.1 23.6 %fusion.13 = f32[4,8,8,9,704]{4,3,1,0,2:T(8,128)} fusion(bf16[4,8,8,9,2048]{4,3,1,0,2:T(8,128)(2,1)} %bitcast.71, bf16[8,2048,352]{1,2,0:T(8,128)(2,1)} %param.11, bf16[8,2048,352]{1,2,0:T(8,128)(2,1)} %param.10), kind=kOutput, calls=%fused_computation.22 | convolution fusion | flops 6689914880 | bytes 38993920 | tf_op jit(solution)/shard_map/abecd,edh->abech/dot_general | solution.py:57
  253.8 131.9 %all-gather.7.cloned.1.call-done = bf16[32,8,9,2048]{3,1,2,0:T(8,128)(2,1)} async-done(((bf16[8,8,9,2048]{3,1,2,0:T(8,128)(2,1)}), bf16[32,8,9,2048]{3,1,2,0:T(8,128)(2,1)}) %all-gather.7.cloned.1.call-update) | async-done | bytes 9437200 | tf_op jit(solution)/shard_map/all_gather | solution.py:38
  385.7 10.7 %copy.50 = bf16[32,8,9,2048]{3,2,0,1:T(8,128)(2,1)} copy(bf16[32,8,9,2048]{3,1,2,0:T(8,128)(2,1)} %all-gather.7.cloned.1.call-done) | data formatting | bytes 18874368 | tf_op jit(solution)/shard_map/all_gather | solution.py:38
  396.4 23.7 %fusion.10 = (bf16[4,8,8,9,352]{4,3,1,0,2:T(8,128)(2,1)}, bf16[4,8,8,9,352]{4,3,1,0,2:T(8,128)(2,1)}) fusion(f32[4,8,8,9,704]{4,3,1,0,2:T(8,128)} %fusion.13, bf16[4,8,8,9,2048]{4,3,1,0,2:T(8,128)(2,1)} %bitcast.70, bf16[8,352,2048]{2,1,0:T(8,128)(2,1)} %param.12), kind=kOutput, calls=%fused_computation.17 | convolution fusion | flops 3332431872 | bytes 30703616 | tf_op jit(solution)/shard_map/abecd,ehd->abech/dot_general | solution.py:85
  420.1 22.6 %convert_bitcast_fusion = bf16[4,8,8,9,2048]{4,3,1,0,2:T(8,128)(2,1)} fusion(bf16[8,2048,352]{1,2,0:T(8,128)(2,1)} %param.11, bf16[8,2048,352]{1,2,0:T(8,128)(2,1)} %param.10, bf16[4,8,8,9,352]{4,3,1,0,2:T(8,128)(2,1)} %get-tuple-element.4, bf16[4,8,8,9,352]{4,3,1,0,2:T(8,128)(2,1)} %get-tuple-element.3), kind=kOutput, calls=%fused_computation.3 | convolution fusion | flops 6701121536 | bytes 35749888 | tf_op jit(solution)/shard_map/abech,edh->abecd/dot_general | solution.py:98
  442.7 13.4 %copy.51 = bf16[4,8,8,9,2048]{4,2,3,1,0:T(8,128)(2,1)} copy(bf16[4,8,8,9,2048]{4,3,1,0,2:T(8,128)(2,1)} %convert_bitcast_fusion) | data formatting | bytes 18874368 | tf_op jit(solution)/shard_map/convert_element_type | solution.py:42
  456.1 17.9 %convert_bitcast_fusion.1 = bf16[4,8,8,9,2048]{4,3,1,0,2:T(8,128)(2,1)} fusion(bf16[8,352,2048]{2,1,0:T(8,128)(2,1)} %param.12, f32[4,8,8,9,704]{4,3,1,0,2:T(8,128)} %fusion.13), kind=kOutput, calls=%fused_computation.4 | convolution fusion | flops 3331473408 | bytes 27459584 | tf_op jit(solution)/shard_map/abech,ehd->abecd/dot_general | solution.py:67
  474.0 13.2 %copy.46 = bf16[4,8,8,9,2048]{4,2,3,1,0:T(8,128)(2,1)} copy(bf16[4,8,8,9,2048]{4,3,1,0,2:T(8,128)(2,1)} %convert_bitcast_fusion.1) | data formatting | bytes 18874368 | tf_op jit(solution)/shard_map/convert_element_type | solution.py:42
  487.3 128.4 %reduce-scatter.5.cloned.1.call-done = bf16[1,8,8,9,2048]{4,2,3,1,0:T(8,128)(2,1)} async-done(((bf16[4,8,8,9,2048]{4,2,3,1,0:T(8,128)(2,1)}), bf16[1,8,8,9,2048]{4,2,3,1,0:T(8,128)(2,1)}) %reduce-scatter.5.cloned.1.call-update) | async-done | bytes 2359312 | tf_op jit(solution)/shard_map/reduce_scatter | solution.py:41
  615.7 3.7 all-to-all-start.3
  619.4 160.7 %reduce-scatter.3.cloned.1.call-done = bf16[1,8,8,9,2048]{4,2,3,1,0:T(8,128)(2,1)} async-done(((bf16[4,8,8,9,2048]{4,2,3,1,0:T(8,128)(2,1)}), bf16[1,8,8,9,2048]{4,2,3,1,0:T(8,128)(2,1)}) %reduce-scatter.3.cloned.1.call-update) | async-done | bytes 2359312 | tf_op jit(solution)/shard_map/reduce_scatter | solution.py:41
  780.0 4.6 all-to-all-start.1
  784.7 0.1 mul.85
  784.8 3.6 copy.52
  788.4 3.4 reshape.101
  791.8 3.3 gather_fusion.1
  795.1 4.1 reshape.102
  799.3 14.9 %all-to-all-done.1 = bf16[8,8,9,2048]{3,1,2,0:T(8,128)(2,1)} async-done(((bf16[8,8,9,2048]{3,1,2,0:T(8,128)(2,1)}), bf16[8,8,9,2048]{3,1,2,0:T(8,128)(2,1)}, u32[]{:S(2)}, u32[]{:S(2)}) %all-to-all-start.1) | async-done | bytes 2359328 | tf_op jit(solution)/shard_map/all_to_all | solution.py:47
  814.1 5.4 copy.47
  819.6 3.4 reshape.98
  823.0 3.3 gather_fusion
  826.3 4.4 reshape.99
  830.8 5.9 multiply_reduce_fusion
  836.6 4.4 fusion.17
  841.0 0.7 copy.56
  841.7 3.9 reduce_sum.51
  (39 shorter events, 0.6 us)
Async XLA Ops:
  7.2 3.7 copy-start
  7.2 212.0 %all-gather.5.cloned.1.call-start = ((), (), s32[]{:S(2)}) async-start(), calls=%async_computation.8 | async-start | bytes 11796480 | tf_op jit(solution)/shard_map/all_gather | solution.py:38
  9.9 51.7 %copy-start.8 = (s32[512]{0:T(512)}, s32[512]{0:T(512)S(1)}, u32[]{:S(2)}) copy-start(s32[512]{0:T(512)S(1)} %fusion.23) | copy-start | bytes 6148
  14.5 38.4 %copy-start.10 = (f32[128,4]{0,1:T(4,128)S(1)}, f32[128,4]{0,1:T(4,128)}, u32[]{:S(2)}) copy-start(f32[128,4]{0,1:T(4,128)} %param.9) | copy-start | bytes 6148
  14.5 38.7 %copy-start.5 = (bf16[128,2048]{1,0:T(8,128)(2,1)S(1)}, bf16[128,2048]{1,0:T(8,128)(2,1)}, u32[]{:S(2)}) copy-start(bf16[128,2048]{1,0:T(8,128)(2,1)} %param.13) | copy-start | bytes 1572868
  52.8 332.9 %all-gather.7.cloned.1.call-start = ((), (), s32[]{:S(2)}) async-start(), calls=%async_computation.9 | async-start | bytes 11796480 | tf_op jit(solution)/shard_map/all_gather | solution.py:38
  53.0 8.6 %copy-start.3 = (f32[128,4]{1,0:T(8,128)}, f32[128,4]{1,0:T(8,128)S(1)}, u32[]{:S(2)}) copy-start(f32[128,4]{1,0:T(8,128)S(1)} %copy.38) | copy-start | bytes 6148
  104.9 510.8 %reduce-scatter.5.cloned.1.call-start = ((), (), s32[]{:S(2)}) async-start(), calls=%async_computation.7 | async-start | bytes 11796480 | tf_op jit(solution)/shard_map/reduce_scatter | solution.py:41
  456.1 324.0 %reduce-scatter.3.cloned.1.call-start = ((), (), s32[]{:S(2)}) async-start(), calls=%async_computation.6 | async-start | bytes 11796480 | tf_op jit(solution)/shard_map/reduce_scatter | solution.py:41
  487.2 297.4 %copy-start.7 = (s32[128,4]{1,0:T(8,128)S(1)}, s32[128,4]{1,0:T(8,128)}, u32[]{:S(2)}) copy-start(s32[128,4]{1,0:T(8,128)} %get-tuple-element.5) | copy-start | bytes 6148
  487.2 297.5 %copy-start.9 = (s32[512]{0:T(512)S(1)}, s32[512]{0:T(512)}, u32[]{:S(2)}) copy-start(s32[512]{0:T(512)} %copy-done.8) | copy-start | bytes 6148
  615.7 164.3 %all-to-all-start.3 = ((bf16[8,8,9,2048]{3,1,2,0:T(8,128)(2,1)}), bf16[8,8,9,2048]{3,1,2,0:T(8,128)(2,1)S(1)}, u32[]{:S(2)}, u32[]{:S(2)}) async-start(bf16[8,8,9,2048]{3,1,2,0:T(8,128)(2,1)} %bitcast.73), calls=%async_computation.5 | async-start | bytes 4718592 | tf_op jit(solution)/shard_map/all_to_all | solution.py:47
  780.0 34.1 %all-to-all-start.1 = ((bf16[8,8,9,2048]{3,1,2,0:T(8,128)(2,1)}), bf16[8,8,9,2048]{3,1,2,0:T(8,128)(2,1)}, u32[]{:S(2)}, u32[]{:S(2)}) async-start(bf16[8,8,9,2048]{3,1,2,0:T(8,128)(2,1)} %bitcast.72), calls=%async_computation.2 | async-start | bytes 4718592 | tf_op jit(solution)/shard_map/all_to_all | solution.py:47
  823.0 7.8 copy-start.4
  826.3 10.3 %copy-start.6 = (bf16[128,2048]{1,0:T(8,128)(2,1)S(1)}, bf16[128,2048]{1,0:T(8,128)(2,1)}, u32[]{:S(2)}) copy-start(bf16[128,2048]{1,0:T(8,128)(2,1)} %param.13) | copy-start | bytes 1572868
  830.8 11.0 %copy-start.2 = (bf16[128,4,2048]{2,1,0:T(4,128)(2,1)S(1)}, bf16[128,4,2048]{2,1,0:T(4,128)(2,1)}, u32[]{:S(2)}) copy-start(bf16[128,4,2048]{2,1,0:T(4,128)(2,1)} %reshape.102) | copy-start | bytes 6291460
  830.8 14.8 %copy-start.1 = (bf16[128,2048]{1,0:T(8,128)(2,1)S(1)}, bf16[128,2048]{1,0:T(8,128)(2,1)}, u32[]{:S(2)}) copy-start(bf16[128,2048]{1,0:T(8,128)(2,1)} %param.7) | copy-start | bytes 1572868
Sparse Core Ops, SparseCore 0:
  53.0 166.1 all-gather.4
  220.7 164.9 all-gather.6
  456.2 159.4 reduce-scatter.4
  617.9 162.0 reduce-scatter.2
where the time goes:
time: 860 us; the launch traced here: 853 us
  waiting for transfers between devices  550 us (64%)
  local copies, waits for them, and re-layouts  103 us (12%)
  matrix products  97 us (11%)
  blocking collectives  67.1 us (8%)
  between operations  14.5 us (2%)
  other arithmetic  11.9 us (1%)
  starting transfers between devices  8.61 us (1%)
    reduce_scatter x2, waiting for transfers between devices, combine(): lax.psum_scatter(term_fn(jnp.int32(0), 1 * lax.axis_size('local')).astype...  289 us
    all_gather x2, waiting for transfers between devices, dispatch(): lax.all_gather(arrived[None], 'local', axis=0, tiled=True)  246 us
    all_to_all x2, blocking collectives, dispatch(): lax.all_to_all(outgoing, 'node', split_axis=0, concat_axis=0, tiled=True)  67.1 us
    convert_element_type x2, local copies, waits for them, and re-layouts, combine(): term_fn(jnp.int32(0), 1 * lax.axis_size('local')).astype(jnp.bfloat16)  26.6 us
    dot_general x1, matrix products, backward_work(): jnp.einsum('abecd,ehd->abech', block_rows, full_down, preferred_element_t...  23.7 us
    dot_general x1, matrix products, forward_work(): jnp.einsum('abecd,edh->abech', block_rows, w_inner, preferred_element_typ...  23.6 us
    dot_general x1, matrix products, back_term(): jnp.einsum('abech,edh->abecd', d_inner, w_inner, preferred_element_type=j...  22.6 us
    all_gather x2, local copies, waits for them, and re-layouts, dispatch(): lax.all_gather(arrived[None], 'local', axis=0, tiled=True)  21.7 us
  transfers between devices with their start and end apart: 6, of which 5 were waited for; matrix products, arithmetic and copies ran while one was open for 12% of the time, Pallas kernels for 0%

commit v1 on v0

--- a/solution.py
+++ b/solution.py
@@ -1,6 +1,10 @@
+import functools
+
 import jax
 import jax.numpy as jnp
 from jax import lax
+from jax.experimental import pallas as pl
+from jax.experimental.pallas import tpu as pltpu
 from jax.sharding import PartitionSpec as P
 
 EXPERTS = 64
@@ -18,7 +22,7 @@
     return flat_routes * CAP + slot_rank
 
 
-def shards(tokens, route, combine_weights, w_gate, w_up, w_down, grad_out):
+def routed_plan(tokens, route, combine_weights, w_gate, w_up, w_down, grad_out):
     node_count = lax.axis_size("node")
     tok_rows, model_width = tokens.shape
     per_node = w_gate.shape[0]
@@ -102,6 +106,441 @@
     d_tokens = jnp.sum(d_pairs.astype(jnp.float32), axis=1).astype(jnp.bfloat16)
     return (combined, d_tokens, d_weights)
 
+MESH = pl.DeviceIdType.MESH
+VMEM_LIMIT = 58 * 1024 * 1024
+F32 = jnp.float32
+BF16 = jnp.bfloat16
+
+
+def place(nodes):
+    n, z = lax.axis_index("node"), lax.axis_index("local")
+    y, x, c = n // (nodes // 2), (n // (nodes // 4)) % 2, n % 2
+    step_x = (nodes // 4) * (1 - 2 * x)
+    step_y = (nodes // 2) * (1 - 2 * y)
+    first = step_x * (1 - c) + step_y * c
+    second = step_x * c + step_y * (1 - c)
+    return n, z, 1 - 2 * c, first, second
+
+
+def greet(n, z, locals_, steps):
+    barrier = pltpu.get_barrier_semaphore()
+    for step in steps:
+        pl.semaphore_signal(barrier, inc=1, device_id=(n + step, z), device_id_type=MESH)
+    for i in range(1, locals_):
+        pl.semaphore_signal(
+            barrier, inc=1, device_id=(n, (z + i) % locals_), device_id_type=MESH
+        )
+    pl.semaphore_wait(barrier, len(steps) + locals_ - 1)
+
+
+def match_rows(meta, k, base, rows):
+    ids = lax.broadcasted_iota(jnp.int32, (rows, meta.shape[1]), 0).astype(F32) + base
+    return ids == meta[k : k + 1, :]
+
+
+def gather_kernel(
+    nodes, locals_, meta_ref, tok_ref, grad_ref, x_ref, g_ref, metas_ref, wr_ref,
+    held, metas, pick, stage, own_sem, send_sem, recv_sem, stage_sem,
+):
+    n, z, sib, first, second = place(nodes)
+    rows = x_ref.shape[1]
+    base = (n * rows).astype(F32)
+    loads = []
+    me = n * locals_ + z
+    for t, src in ((0, meta_ref), (1, tok_ref), (2, grad_ref)):
+        dst = metas.at[me] if t == 0 else held.at[t - 1, me]
+        copy = pltpu.make_async_copy(src, dst, own_sem.at[t])
+        copy.start()
+        loads.append(copy)
+    greet(n, z, locals_, (sib, first, second))
+
+    def block(t, index):
+        return metas.at[index] if t == 0 else held.at[t - 1, index]
+
+    def copy_of(t, index, slot, node, local):
+        return pltpu.make_async_remote_copy(
+            src_ref=block(t, index),
+            dst_ref=block(t, index),
+            send_sem=send_sem.at[t, slot],
+            recv_sem=recv_sem.at[t, index],
+            device_id=(node, local),
+            device_id_type=MESH,
+        )
+
+    def arrived(t, index):
+        copy_of(t, index, 0, n + sib, z).wait_recv()
+
+    def at(step, i):
+        return (n + step) * locals_ + (z + locals_ - i) % locals_
+
+    slots = iter(range(3 * 64))
+    counts = [0, 0, 0]
+
+    def send(t, index, node, local):
+        copy_of(t, index, counts[t], node, local).start()
+        counts[t] += 1
+
+    def phase_own(t):
+        loads[t].wait()
+        for i in range(1, locals_):
+            send(t, me, n, (z + i) % locals_)
+        send(t, me, n + second, z)
+        send(t, me, n + first, z)
+        send(t, me, n + sib, z)
+
+    def phase_local(t):
+        for i in range(1, locals_):
+            index = at(0, i)
+            arrived(t, index)
+            send(t, index, n + second, z)
+            send(t, index, n + first, z)
+            send(t, index, n + sib, z)
+
+    def phase_first(t):
+        for i in range(locals_):
+            index = at(first, i)
+            arrived(t, index)
+            send(t, index, n + second, z)
+            send(t, index, n + sib, z)
+
+    def phase_second(t, step):
+        for i in range(locals_):
+            index = at(step, i)
+            arrived(t, index)
+            send(t, index, n + sib, z)
+
+    def from_sibling(t, step):
+        for i in range(locals_):
+            arrived(t, at(step, i))
+
+    def dispatch(t, step, out_ref, order):
+        group = n + step
+        width = held.shape[2]
+        for l in range(locals_):
+            meta = metas[group * locals_ + l]
+            hit = match_rows(meta, 0, base, rows)
+            weight = jnp.where(hit, meta[TOP : TOP + 1, :], 0.0)
+            for k in range(1, TOP):
+                hit_k = match_rows(meta, k, base, rows)
+                weight = jnp.where(hit_k, meta[TOP + k : TOP + k + 1, :], weight)
+                hit = hit | hit_k
+            pick[:, l * width : (l + 1) * width] = jnp.where(hit, 1.0, 0.0).astype(BF16)
+            if t == 2:
+                total = jnp.sum(weight, axis=1, keepdims=True)
+                total = jnp.broadcast_to(total, (rows, wr_ref.shape[2]))
+                if l == 0:
+                    wr_ref[group] = total
+                else:
+                    wr_ref[group] = wr_ref[group] + total
+        slot = order % 2
+        out = pltpu.make_async_copy(stage.at[slot], out_ref.at[group], stage_sem.at[slot])
+        if order >= 2:
+            out.wait()
+        tile = 512
+
+        def columns(j, carry):
+            cols = pl.ds(pl.multiple_of(j * tile, tile), tile)
+            data = held[t - 1, pl.ds(group * locals_, locals_), :, cols]
+            data = data.reshape(locals_ * width, tile)
+            stage[slot, :, cols] = jnp.dot(
+                pick[...], data, preferred_element_type=F32
+            ).astype(BF16)
+            return carry
+
+        lax.fori_loop(0, held.shape[3] // tile, columns, 0)
+        out.start()
+
+    steps = (0, first, second, first + second)
+    other = (sib, sib + second, sib + first, sib + first + second)
+    phase_own(0)
+    phase_own(1)
+    phase_own(2)
+    phase_local(0)
+    phase_first(0)
+    phase_local(1)
+    phase_second(0, second)
+    phase_second(0, first + second)
+    for step in other:
+        from_sibling(0, step)
+    phase_first(1)
+    phase_local(2)
+    dispatch(1, 0, x_ref, 0)
+    phase_second(1, second)
+    phase_first(2)
+    phase_second(1, first + second)
+    from_sibling(1, other[0])
+    dispatch(1, first, x_ref, 1)
+    dispatch(1, second, x_ref, 2)
+    dispatch(1, other[0], x_ref, 3)
+    for j in range(1, 4):
+        from_sibling(1, other[j])
+    dispatch(1, first + second, x_ref, 4)
+    dispatch(1, other[1], x_ref, 5)
+    phase_second(2, second)
+    dispatch(1, other[2], x_ref, 6)
+    dispatch(1, other[3], x_ref, 7)
+    dispatch(2, 0, g_ref, 8)
+    dispatch(2, first, g_ref, 9)
+    dispatch(2, second, g_ref, 10)
+    from_sibling(2, other[0])
+    dispatch(2, other[0], g_ref, 11)
+    phase_second(2, first + second)
+    from_sibling(2, other[1])
+    from_sibling(2, other[2])
+    dispatch(2, other[1], g_ref, 12)
+    dispatch(2, other[2], g_ref, 13)
+    dispatch(2, first + second, g_ref, 14)
+    from_sibling(2, other[3])
+    dispatch(2, other[3], g_ref, 15)
+    metas_ref[...] = metas[...]
+    for slot, order in ((0, 14), (1, 15)):
+        pltpu.make_async_copy(stage.at[slot], g_ref.at[n], stage_sem.at[slot]).wait()
+    for t in range(3):
+        for s in range(counts[t]):
+            copy_of(t, me, s, n + sib, z).wait_send()
+
+
+def expert_kernel(x_ref, g_ref, wr_ref, wg_ref, wu_ref, wd_ref, y_ref, b_ref, dw_ref):
+    groups, cap, width = x_ref.shape
+    rows = groups * cap
+    contract_last = (((1,), (1,)), ((), ()))
+    x = x_ref[...].reshape(rows, width)
+    g = g_ref[...].reshape(rows, width)
+    w = wr_ref[...].reshape(rows, wr_ref.shape[2])[:, 0:1]
+    gate = jnp.dot(x, wg_ref[0], preferred_element_type=F32)
+    up = jnp.dot(x, wu_ref[0], preferred_element_type=F32)
+    pull = lax.dot_general(g, wd_ref[0], contract_last, preferred_element_type=F32)
+    s = 1.0 / (1.0 + jnp.exp(-gate))
+    hidden = gate * s * up
+    dw = jnp.sum(hidden.astype(BF16).astype(F32) * pull, axis=1, keepdims=True)
+    dw_ref[...] = jnp.broadcast_to(dw, (rows, dw_ref.shape[2])).reshape(dw_ref.shape)
+    pull = pull * w
+    d_gate = (pull * up * s * (1.0 + gate * (1.0 - s))).astype(BF16)
+    d_up = (pull * gate * s).astype(BF16)
+    y = jnp.dot((hidden * w).astype(BF16), wd_ref[0], preferred_element_type=F32)
+    y_ref[...] = y.astype(BF16).reshape(y_ref.shape)
+    back = lax.dot_general(d_gate, wg_ref[0], contract_last, preferred_element_type=F32)
+    back += lax.dot_general(d_up, wu_ref[0], contract_last, preferred_element_type=F32)
+    b_ref[...] = back.astype(BF16).reshape(b_ref.shape)
+
+
+def reduce_kernel(
+    nodes, locals_, metas_ref, y_ref, out_ref,
+    rows_in, pick, sib_send, sib_recv, hop_send, hop_recv, end_send, end_recv,
+    load_sem, sib_sems, hop_sems, end_sems,
+):
+    n, z, sib, first, second = place(nodes)
+    rows, model_width = y_ref.shape[1], y_ref.shape[2]
+    width = out_ref.shape[0]
+    base = (n * rows).astype(F32)
+    order = (
+        sib + first + second, sib + first, sib + second, sib,
+        first + second, second, first, 0,
+    )
+
+    def load(j):
+        return pltpu.make_async_copy(
+            y_ref.at[n + order[j]], rows_in.at[j % 2], load_sem.at[j % 2]
+        )
+
+    load(0).start()
+    greet(n, z, locals_, (sib, first, second))
+    tile = 512
+    tiles = model_width // tile
+
+    def copy_to(src, dst, sems, s, node, local):
+        return pltpu.make_async_remote_copy(
+            src_ref=src,
+            dst_ref=dst,
+            send_sem=sems.at[0, s],
+            recv_sem=sems.at[1, s],
+            device_id=(node, local),
+            device_id_type=MESH,
+        )
+
+    def sib_copy(j, l):
+        s = j * locals_ + l
+        return copy_to(sib_send.at[s], sib_recv.at[s], sib_sems, s, n + sib, z)
+
+    def hop_copy(j, l):
+        s = j * locals_ + l
+        step = second if j < 2 else first
+        return copy_to(hop_send.at[s], hop_recv.at[s], hop_sems, s, n + step, z)
+
+    def end_copy(i):
+        return copy_to(
+            end_send.at[i], end_recv.at[i], end_sems, i, n, (z + i) % locals_
+        )
+
+    def part(j, l, addends, dst):
+        meta = metas_ref[(n + order[j]) * locals_ + l]
+        hit = match_rows(meta, 0, base, rows)
+        for k in range(1, TOP):
+            hit = hit | match_rows(meta, k, base, rows)
+        pick[...] = jnp.where(hit, 1.0, 0.0).astype(BF16)
+
+        def columns(q, carry):
+            cols = pl.ds(pl.multiple_of(q * tile, tile), tile)
+            total = lax.dot_general(
+                pick[...], rows_in[j % 2, :, cols], (((0,), (0,)), ((), ())),
+                preferred_element_type=F32,
+            )
+            for ref in addends:
+                total = total + ref[:, cols].astype(F32)
+            dst[:, cols] = total.astype(BF16)
+            return carry
+
+        lax.fori_loop(0, tiles, columns, 0)
+
+    for j in range(8):
+        load(j).wait()
+        if j + 1 < 8:
+            load(j + 1).start()
+        for i in range(locals_):
+            l = (z + i) % locals_
+            m = i
+            if j < 4:
+                part(j, l, [], sib_send.at[j * locals_ + m])
+                sib_copy(j, m).start()
+                continue
+            s = (j - 4) * locals_ + m
+            sib_copy(j - 4, m).wait_recv()
+            addends = [sib_recv.at[s]]
+            if j == 6:
+                hop_copy(0, m).wait_recv()
+                addends.append(hop_recv.at[m])
+            if j == 7:
+                hop_copy(1, m).wait_recv()
+                hop_copy(2, m).wait_recv()
+                addends.append(hop_recv.at[locals_ + m])
+                addends.append(hop_recv.at[2 * locals_ + m])
+            if j < 7:
+                part(j, l, addends, hop_send.at[s])
+                hop_copy(j - 4, m).start()
+            else:
+                part(j, l, addends, end_send.at[m])
+                if i > 0:
+                    end_copy(i).start()
+    for i in range(1, locals_):
+        end_copy(i).wait_recv()
+
+    def finish(q, carry):
+        cols = pl.ds(pl.multiple_of(q * tile, tile), tile)
+        total = end_send[0, :, cols].astype(F32)
+        for i in range(1, locals_):
+            total = total + end_recv[i, :, cols].astype(F32)
+        out_ref[:, cols] = total.astype(BF16)
+        return carry
+
+    lax.fori_loop(0, tiles, finish, 0)
+    for j in range(4):
+        for m in range(locals_):
+            sib_copy(j, m).wait_send()
+    for j in range(3):
+        for m in range(locals_):
+            hop_copy(j, m).wait_send()
+    for i in range(1, locals_):
+        end_copy(i).wait_send()
+
+
+def gathered_plan(tokens, route, combine_weights, w_gate, w_up, w_down, grad_out):
+    nodes, locals_ = lax.axis_size("node"), lax.axis_size("local")
+    tok_rows, model_width = tokens.shape
+    per_node, _, hidden_width = w_gate.shape
+    devices = nodes * locals_
+    cap = -(-(locals_ * CAP) // 16) * 16
+    rows = per_node * cap
+    place_at = place_pairs(route)
+    flat = route.reshape(-1)
+    slot = place_at - flat * CAP
+    row_id = flat * cap + lax.axis_index("local") * CAP + slot
+    meta = jnp.concatenate(
+        [row_id.reshape(tok_rows, TOP).T.astype(F32), combine_weights.T], axis=0
+    )
+    any_space = pl.BlockSpec(memory_space=pl.ANY)
+    vmem_space = pl.BlockSpec(memory_space=pltpu.VMEM)
+    x_rows, g_rows, metas, row_weights = pl.pallas_call(
+        functools.partial(gather_kernel, nodes, locals_),
+        out_shape=(
+            jax.ShapeDtypeStruct((nodes, rows, model_width), BF16),
+            jax.ShapeDtypeStruct((nodes, rows, model_width), BF16),
+            jax.ShapeDtypeStruct((devices, 2 * TOP, tok_rows), F32),
+            jax.ShapeDtypeStruct((nodes, rows, 128), F32),
+        ),
+        in_specs=[any_space] * 3,
+        out_specs=(any_space, any_space, vmem_space, vmem_space),
+        scratch_shapes=[
+            pltpu.VMEM((2, devices, tok_rows, model_width), BF16),
+            pltpu.VMEM((devices, 2 * TOP, tok_rows), F32),
+            pltpu.VMEM((rows, locals_ * tok_rows), BF16),
+            pltpu.VMEM((2, rows, model_width), BF16),
+            pltpu.SemaphoreType.DMA((3,)),
+            pltpu.SemaphoreType.DMA((3, devices)),
+            pltpu.SemaphoreType.DMA((3, devices)),
+            pltpu.SemaphoreType.DMA((2,)),
+        ],
+        compiler_params=pltpu.CompilerParams(
+            collective_id=0, has_side_effects=True, vmem_limit_bytes=VMEM_LIMIT
+        ),
+    )(meta, tokens, grad_out)
+
+    row_block = pl.BlockSpec((nodes, cap, model_width), lambda e: (0, e, 0))
+    scalar_block = pl.BlockSpec((nodes, cap, 128), lambda e: (0, e, 0))
+    tall = pl.BlockSpec((1, model_width, hidden_width), lambda e: (e, 0, 0))
+    wide = pl.BlockSpec((1, hidden_width, model_width), lambda e: (e, 0, 0))
+    y_rows, b_rows, d_row_weights = pl.pallas_call(
+        expert_kernel,
+        grid=(per_node,),
+        out_shape=(
+            jax.ShapeDtypeStruct((nodes, rows, model_width), BF16),
+            jax.ShapeDtypeStruct((nodes, rows, model_width), BF16),
+            jax.ShapeDtypeStruct((nodes, rows, 128), F32),
+        ),
+        in_specs=[row_block, row_block, scalar_block, tall, tall, wide],
+        out_specs=(row_block, row_block, scalar_block),
+        compiler_params=pltpu.CompilerParams(vmem_limit_bytes=VMEM_LIMIT),
+    )(x_rows, g_rows, row_weights, w_gate, w_up, w_down)
+
+    reduce_call = pl.pallas_call(
+        functools.partial(reduce_kernel, nodes, locals_),
+        out_shape=jax.ShapeDtypeStruct((tok_rows, model_width), BF16),
+        in_specs=[vmem_space, any_space],
+        out_specs=vmem_space,
+        scratch_shapes=[
+            pltpu.VMEM((2, rows, model_width), BF16),
+            pltpu.VMEM((rows, tok_rows), BF16),
+            pltpu.VMEM((4 * locals_, tok_rows, model_width), BF16),
+            pltpu.VMEM((4 * locals_, tok_rows, model_width), BF16),
+            pltpu.VMEM((3 * locals_, tok_rows, model_width), BF16),
+            pltpu.VMEM((3 * locals_, tok_rows, model_width), BF16),
+            pltpu.VMEM((locals_, tok_rows, model_width), BF16),
+            pltpu.VMEM((locals_, tok_rows, model_width), BF16),
+            pltpu.SemaphoreType.DMA((2,)),
+            pltpu.SemaphoreType.DMA((2, 4 * locals_)),
+            pltpu.SemaphoreType.DMA((2, 3 * locals_)),
+            pltpu.SemaphoreType.DMA((2, locals_)),
+        ],
+        compiler_params=pltpu.CompilerParams(
+            collective_id=1, has_side_effects=True, vmem_limit_bytes=VMEM_LIMIT
+        ),
+    )
+    ids = metas[:, :TOP, :].reshape(nodes, locals_ * TOP * tok_rows)
+    local_row = ids.astype(jnp.int32) - lax.axis_index("node") * rows
+    named = local_row[:, :, None] == jnp.arange(rows, dtype=jnp.int32)[None, None, :]
+    parts = jnp.sum(jnp.where(named, d_row_weights[:, None, :, 0], 0.0), axis=2)
+    d_weights = lax.psum_scatter(
+        parts.reshape(devices, TOP, tok_rows), ("node", "local"), scatter_dimension=0, tiled=True
+    )[0].T
+    combined = reduce_call(metas, y_rows)
+    d_tokens = reduce_call(metas, b_rows)
+    return (combined, d_tokens, d_weights)
+
+
+def shards(tokens, *rest):
+    if lax.axis_size("node") == 2 * TOP:
+        return gathered_plan(tokens, *rest)
+    return routed_plan(tokens, *rest)
+
 
 def solution(mesh):
     return jax.shard_map(

time: 860 us -> 546 us (0.63)
  waiting for transfers between devices: 550 us -> 0.04 us
  Pallas kernels: 0 us -> 476 us
  matrix products: 97 us -> 0 us
  blocking collectives: 67.1 us -> 0 us
  local copies, waits for them, and re-layouts: 103 us -> 38.8 us
    pallas_call x0 -> x4, Pallas kernels: none -> 476 us  [the longest x1 167 us: gathered_plan(): pl.pallas_call(functools.partial(gather_kernel, nodes, locals_), out_shap...]
    reduce_scatter x2 -> x0, waiting for transfers between devices: 289 us -> none  [combine(): lax.psum_scatter(term_fn(jnp.int32(0), 1 * lax.axis_size('local')).astype...]
    all_gather x2 -> x0, waiting for transfers between devices: 246 us -> none  [dispatch(): lax.all_gather(arrived[None], 'local', axis=0, tiled=True)]
    dot_general x7 -> x0, matrix products: 97 us -> none  [the longest x1 23.7 us: backward_work(): jnp.einsum('abecd,ehd->abech', block_rows, full_down, preferred_element_t...]
    all_to_all x2 -> x0, blocking collectives: 67.1 us -> none  [dispatch(): lax.all_to_all(outgoing, 'node', split_axis=0, concat_axis=0, tiled=True)]
    unnamed x24 -> x13, local copies, waits for them, and re-layouts: 1.01 us -> 34.4 us
    reshape x8 -> x1, local copies, waits for them, and re-layouts: 28.6 us -> 0.68 us  [gathered_plan(): parts.reshape(devices, TOP, tok_rows)]
    convert_element_type x2 -> x0, local copies, waits for them, and re-layouts: 26.6 us -> none  [combine(): term_fn(jnp.int32(0), 1 * lax.axis_size('local')).astype(jnp.bfloat16)]
  transfers between devices with their start and end apart: 6 -> 1, of which waited for: 5 -> 0; matrix products, arithmetic and copies ran while one was open for 12% -> 0% of each run, Pallas kernels for 0% -> 49%
where the time goes in v1:
time: 546 us; the launch traced here: 537 us
  Pallas kernels  476 us (87%)
  local copies, waits for them, and re-layouts  38.8 us (7%)
  between operations  14.2 us (3%)
  other arithmetic  7.62 us (1%)
    pallas_call x1, Pallas kernels, gathered_plan(): pl.pallas_call(functools.partial(gather_kernel, nodes, locals_), out_shap...  167 us
    pallas_call x1, Pallas kernels, gathered_plan(): combined = reduce_call(metas, y_rows)  131 us
    pallas_call x1, Pallas kernels, gathered_plan(): d_tokens = reduce_call(metas, b_rows)  130 us
    pallas_call x1, Pallas kernels, gathered_plan(): pl.pallas_call(expert_kernel, grid=(per_node,), out_shape=(jax.ShapeDtype...  47 us
    unnamed x13, local copies, waits for them, and re-layouts  34.4 us
  transfers between devices with their start and end apart: 1, of which 0 were waited for; matrix products, arithmetic and copies ran while one was open for 0% of the time, Pallas kernels for 49%

profile of v1, /device:TPU:0, one launch (start us, length us, event | category | flops | bytes accessed | tf_op | source)
XLA Modules:
  0.0 536.8 jit_solution(553798300268678944)
XLA Ops:
  7.2 0.0 all-reduce.3.cloned.1.call-start
  7.2 0.8 copy.24
  8.0 0.1 eq.38
  8.1 0.1 eq.42
  8.2 1.2 reduce-window.6
  9.4 0.2 slice_reduce_fusion.1
  9.7 0.1 fusion.2
  9.8 0.1 reduce_sum.21
  10.0 0.1 copy.27
  10.0 15.4 %copy.28.wg_ref = bf16[8,2048,352]{2,1,0:T(8,128)(2,1)} copy(bf16[8,2048,352]{1,2,0:T(8,128)(2,1)} %param.10) | data formatting | bytes 23068672 | tf_op args[3]
  25.5 0.0 copy-start.2
  25.5 0.0 copy-start.3
  25.5 15.5 %copy.29.wu_ref = bf16[8,2048,352]{2,1,0:T(8,128)(2,1)} copy(bf16[8,2048,352]{1,2,0:T(8,128)(2,1)} %param.11) | data formatting | bytes 23068672 | tf_op args[4]
  40.9 0.0 copy-done.2
  40.9 0.0 copy-done.3
  41.0 0.6 pad_maximum_fusion.meta_ref
  41.6 167.5 %shard_map.94 = (bf16[8,384,2048]{2,1,0:T(8,128)(2,1)}, bf16[8,384,2048]{2,1,0:T(8,128)(2,1)}, f32[32,8,128]{2,1,0:T(8,128)}, f32[8,384,128]{2,1,0:T(8,128)}) custom-call(f32[8,128]{1,0:T(8,128)} %pad_maximum_fusion.meta_ref, bf16[128,2048]{1,0:T(8,128)(2,1)} %tok_ref.1, bf16[128,2048]{1,0:T(8,128)(2,1)} %grad_ref.1), custom_call_target="tpu_custom_call" | custom-call | tf_op jit(solution)/shard_map/pallas_call | solution.py:462
  209.0 0.0 copy-start.1
  209.0 47.0 %shard_map.95 = (bf16[8,384,2048]{2,1,0:T(8,128)(2,1)}, bf16[8,384,2048]{2,1,0:T(8,128)(2,1)}, f32[8,384,128]{2,1,0:T(8,128)}) custom-call(bf16[8,384,2048]{2,1,0:T(8,128)(2,1)} %get-tuple-element.11.x_ref, bf16[8,384,2048]{2,1,0:T(8,128)(2,1)} %get-tuple-element.12.g_ref, f32[8,384,128]{2,1,0:T(8,128)} %get-tuple-element.13.wr_ref, ...), custom_call_target="tpu_custom_call" | custom-call | tf_op jit(solution)/shard_map/pallas_call | solution.py:491
  256.1 1.9 slice_reduce_fusion
  258.0 0.0 copy-done.1
  258.0 5.6 %select_reduce_fusion = f32[8,2048]{1,0:T(8,128)S(1)} fusion(f32[8,384]{1,0:T(8,128)S(1)} %slice_reduce_fusion, s32[8,2048]{1,0:T(8,128)S(1)} %sub.20), kind=kLoop, calls=%fused_computation | loop fusion | flops 18857984 | bytes 143360 | tf_op jit(solution)/shard_map/reduce_sum | solution.py:530
  263.7 0.7 reshape.42
  264.3 0.0 all-reduce.3.cloned.1.call-update
  264.4 131.5 %shard_map.96 = bf16[128,2048]{1,0:T(8,128)(2,1)} custom-call(f32[32,8,128]{2,1,0:T(8,128)} %get-tuple-element.10.metas_ref, bf16[8,384,2048]{2,1,0:T(8,128)(2,1)} %get-tuple-element.14.y_ref), custom_call_target="tpu_custom_call" | custom-call | tf_op jit(solution)/shard_map/pallas_call | solution.py:534
  395.8 0.0 copy-start
  395.9 130.2 %shard_map.97 = bf16[128,2048]{1,0:T(8,128)(2,1)} custom-call(f32[32,8,128]{2,1,0:T(8,128)} %get-tuple-element.10.metas_ref, bf16[8,384,2048]{2,1,0:T(8,128)(2,1)} %get-tuple-element.15.y_ref), custom_call_target="tpu_custom_call" | custom-call | tf_op jit(solution)/shard_map/pallas_call | solution.py:535
  526.1 0.0 all-reduce.3.cloned.1.call-done
  526.1 1.2 dynamic-slice_bitcast_fusion
  527.3 0.0 copy-done
  527.3 0.8 copy.35
  528.1 1.9 copy.36
  (6 shorter events, 0.1 us)
Async XLA Ops:
  7.2 518.9 %all-reduce.3.cloned.1.call-start = ((), (), s32[]{:S(2)}) async-start(), calls=%async_computation | async-start | bytes 131072
  25.5 15.5 %copy-start.2 = (s32[128,4]{0,1:T(4,128)S(1)}, s32[128,4]{0,1:T(4,128)}, u32[]{:S(2)}) copy-start(s32[128,4]{0,1:T(4,128)} %param.8) | copy-start | bytes 6148
  25.5 15.5 %copy-start.3 = (f32[128,4]{0,1:T(4,128)S(1)}, f32[128,4]{0,1:T(4,128)}, u32[]{:S(2)}) copy-start(f32[128,4]{0,1:T(4,128)} %param.9) | copy-start | bytes 6148
  209.0 48.9 %copy-start.1 = (f32[32,8,128]{2,1,0:T(8,128)S(1)}, f32[32,8,128]{2,1,0:T(8,128)}, u32[]{:S(2)}) copy-start(f32[32,8,128]{2,1,0:T(8,128)} %get-tuple-element.10.metas_ref) | copy-start | bytes 393220
  395.8 131.5 %copy-start = (bf16[128,2048]{1,0:T(8,128)(2,1)S(1)}, bf16[128,2048]{1,0:T(8,128)(2,1)}, u32[]{:S(2)}) copy-start(bf16[128,2048]{1,0:T(8,128)(2,1)} %shard_map.96) | copy-start | bytes 1572868
Sparse Core Ops, SparseCore 0:
  264.5 142.9 all-reduce.2
